TPU v7x, 128 devices: a whole 4x4x4 slice. The times are simulated.
128 devices in a mesh: dom: 8 (over z, core), shard: 16 (over y, x).
Axes of the slice: x: 4, y: 4, z: 4, core: 2. Of those that a mesh axis runs over, the one named last changes fastest.
Arguments:
- features: bfloat16 [65536, 512], P(('dom', 'shard')), may hold values from -6 to 6
- tile_values: bfloat16 [128, 48, 128, 128], P(('dom', 'shard')), may hold values from -0.5 to 0.5
- tile_coords: int32 [128, 48, 2], P(('dom', 'shard')), may hold values from 0 to 7, as said below
- tile_count: int32 [128], P(('dom', 'shard')), may hold values from 8 to 48, as said below
- boundary_index: int32 [128, 8], P(('dom', 'shard')), may hold values from 0 to 511
- peer_pick: int32 [128, 128, 4], P(('dom', 'shard')), may hold values from 0 to 7
- shuffle_order: int32 [128, 512], P(('dom', 'shard')), may hold values from 0 to 511, each once within a row
- attn_weight: bfloat16 [1, 4, 512, 512], replicated, may hold values from -0.25 to 0.25
- ffn_in: bfloat16 [1, 512, 1024], replicated, may hold values from -0.25 to 0.25
- ffn_out: bfloat16 [1, 1024, 512], replicated, may hold values from -0.1875 to 0.1875
- norm_gain: float32 [1, 2, 512], replicated, may hold values from 0.1 to 1.9
- read_weight: float32 [2, 512], replicated, may hold values from -0.1875 to 0.1875
Outputs:
- node_states: bfloat16 [65536, 512], P(('dom', 'shard'))
Inputs may be any that keep to these rules, and one draw needn't show every extreme that they name: `tile_coords`: slot r < 4 of every device holds (r, r); slot 4 + j for j < 4 has column block 4 + j; column blocks below 4 are the device's own rows, the others its rows taken from other devices. Slots from tile_count[p] on are unused; some device uses all 48 slots.
All inputs are finite; a program needn't handle non-finite values.
Results may differ from a plain program's by a relative error of at most 0.012.
Values may be sent and summed in bfloat16 or wider, within the bound.
A program may use at most 192 MiB of HBM per device.

v0:
```python
import jax
import jax.numpy as jnp
from jax import lax
from jax.sharding import PartitionSpec as P

HEADS = 8
HOPS = 4


def propagate(current, halo_rows, tile_set, tile_place, live_count):
    feat_width = current.shape[1]
    tile_size = tile_set.shape[1]
    row_tiles = current.shape[0] // tile_size
    sources = jnp.concatenate([current, halo_rows], 0).reshape(-1, tile_size, feat_width)
    picked = sources[tile_place[:, 1]]
    product = jnp.einsum("tab,tbf->taf", tile_set, picked, preferred_element_type=jnp.float32)
    live = (jnp.arange(tile_set.shape[0]) < live_count).astype(jnp.float32)
    selector = (tile_place[:, 0][None, :] == jnp.arange(row_tiles)[:, None]).astype(
        jnp.float32
    ) * live[None, :]
    summed = jnp.einsum("rt,taf->raf", selector, product, precision=lax.Precision.HIGHEST)
    return summed.reshape(-1, feat_width).astype(jnp.bfloat16)


def layer_norm(inputs, gain):
    center = inputs - jnp.mean(inputs, -1, keepdims=True)
    spread = jnp.mean(center * center, -1, keepdims=True)
    return center * lax.rsqrt(spread + 1e-05) * gain


def encode(arrived, attn_weight, ffn_in, ffn_out, norm_gain, read_weight):
    node_count = arrived.shape[0]
    token_count = arrived.shape[1]
    feat_width = arrived.shape[2]
    head_dim = feat_width // HEADS
    hidden = arrived.astype(jnp.float32).reshape(node_count * token_count, feat_width)
    normed = layer_norm(hidden, norm_gain[0, 0]).astype(jnp.bfloat16)
    queries = jnp.dot(normed, attn_weight[0, 0], preferred_element_type=jnp.float32).reshape(
        node_count, token_count, HEADS, head_dim
    )
    key_vecs = jnp.dot(normed, attn_weight[0, 1], preferred_element_type=jnp.float32).reshape(
        node_count, token_count, HEADS, head_dim
    )
    value_vecs = jnp.dot(normed, attn_weight[0, 2], preferred_element_type=jnp.float32).reshape(
        node_count, token_count, HEADS, head_dim
    )
    scores = jnp.einsum(
        "nihd,njhd->nhij", queries, key_vecs, precision=lax.Precision.HIGHEST
    ) * head_dim ** (-0.5)
    weights = jnp.exp(scores)
    weights = weights / jnp.sum(weights, -1, keepdims=True)
    context = jnp.einsum("nhij,njhd->nihd", weights, value_vecs, precision=lax.Precision.HIGHEST)
    context = context.reshape(node_count * token_count, feat_width).astype(jnp.bfloat16)
    hidden = hidden + jnp.dot(context, attn_weight[0, 3], preferred_element_type=jnp.float32)
    normed = layer_norm(hidden, norm_gain[0, 1]).astype(jnp.bfloat16)
    expanded = jax.nn.gelu(
        jnp.dot(normed, ffn_in[0], preferred_element_type=jnp.float32), approximate=True
    ).astype(jnp.bfloat16)
    hidden = hidden + jnp.dot(expanded, ffn_out[0], preferred_element_type=jnp.float32)
    hidden = hidden.reshape(node_count, token_count, feat_width)
    center = hidden[:, 0]
    others = hidden[:, 1:]
    read_score = jnp.dot(center, read_weight[0], precision=lax.Precision.HIGHEST)[
        :, None
    ] + jnp.einsum("nkf,f->nk", others, read_weight[1], precision=lax.Precision.HIGHEST)
    weights = jnp.exp(read_score)
    weights = weights / jnp.sum(weights, -1, keepdims=True)
    return (
        center + jnp.einsum("nk,nkf->nf", weights, others, precision=lax.Precision.HIGHEST)
    ).astype(jnp.bfloat16)


def local(
    features,
    tile_values,
    tile_coords,
    tile_count,
    boundary_index,
    peer_pick,
    shuffle_order,
    attn_weight,
    ffn_in,
    ffn_out,
    norm_gain,
    read_weight,
):
    tile_set = tile_values[0]
    tile_place = tile_coords[0]
    live_count = tile_count[0]
    border = boundary_index[0]
    pick_list = peer_pick[0]
    row_order = shuffle_order[0]
    peer_count = pick_list.shape[0]
    incoming = lax.all_to_all(pick_list, ("dom", "shard"), split_axis=0, concat_axis=0, tiled=True)
    lookup = (
        incoming + jnp.arange(peer_count, dtype=jnp.int32)[:, None] * border.shape[0]
    ).reshape(-1)
    current = features
    hop_list = [features]
    for hop_index in range(HOPS):
        edge_rows = current[border]
        table = lax.all_gather(edge_rows, ("dom", "shard"), axis=0, tiled=True)
        fetched = table[lookup]
        current = propagate(current, fetched, tile_set, tile_place, live_count)
        hop_list.append(current)
    stacked = jnp.stack(hop_list, 1)[row_order]
    flat_rows = stacked.reshape(stacked.shape[0], -1)
    arrived = lax.all_to_all(flat_rows, "shard", split_axis=0, concat_axis=0, tiled=True).reshape(
        stacked.shape
    )
    return encode(arrived, attn_weight, ffn_in, ffn_out, norm_gain, read_weight)


def solution(mesh):
    placed = (
        P(("dom", "shard"), None),
        P(("dom", "shard"), None, None, None),
        P(("dom", "shard"), None, None),
        P(("dom", "shard")),
        P(("dom", "shard"), None),
        P(("dom", "shard"), None, None),
        P(("dom", "shard"), None),
        P(),
        P(),
        P(),
        P(),
        P(),
    )
    return jax.shard_map(
        local, mesh=mesh, in_specs=placed, out_specs=P(("dom", "shard"), None), check_vma=False
    )
```

profile of v0, /device:TPU:1, one launch (start us, length us, event | category | flops | bytes accessed | tf_op | source)
XLA Modules:
  0.0 772.4 jit_solution(15067286276535753678)
XLA Ops:
  11.1 11.5 %all-to-all-start = ((s32[128,1,4]{2,1,0:T(1,128)}), s32[128,1,4]{2,1,0:T(1,128)S(1)}, u32[]{:S(2)}, u32[]{:S(2)}) async-start(s32[128,1,4]{2,1,0:T(1,128)} %bitcast.7), calls=%async_computation | async-start | bytes 131072 | tf_op jit(solution)/shard_map/all_to_all | solution.py:94
  24.3 7.8 %all-to-all-done = s32[128,1,4]{2,1,0:T(1,128)S(1)} async-done(((s32[128,1,4]{2,1,0:T(1,128)}), s32[128,1,4]{2,1,0:T(1,128)S(1)}, u32[]{:S(2)}, u32[]{:S(2)}) %all-to-all-start) | async-done | bytes 2080 | tf_op jit(solution)/shard_map/all_to_all | solution.py:94
  33.5 43.8 %all-gather.9.cloned.1.call-done = bf16[1024,512]{1,0:T(8,128)(2,1)} async-done(((bf16[8,512]{1,0:T(8,128)(2,1)}), bf16[1024,512]{1,0:T(8,128)(2,1)}) %all-gather.9.cloned.1.call-update) | async-done | bytes 1048592 | tf_op jit(solution)/shard_map/all_gather | solution.py:102
  82.5 4.9 gather_fusion.2
  87.4 9.2 %convolution_bitcast_fusion.3 = f32[48,128,512]{1,2,0:T(8,128)} fusion(bf16[48,128,512]{2,1,0:T(8,128)(2,1)} %gather_fusion.2, bf16[1,48,128,128]{3,2,1,0:T(8,128)(2,1)S(1)} %copy-done), kind=kOutput, calls=%fused_computation.38 | convolution fusion | flops 805306368 | bytes 20447232 | tf_op jit(solution)/shard_map/tab,tbf->taf/dot_general | solution.py:16
  96.5 12.7 %copy.126 = f32[48,128,512]{2,0,1:T(8,128)} copy(f32[48,128,512]{1,2,0:T(8,128)} %convolution_bitcast_fusion.3) | data formatting | bytes 25165824 | tf_op jit(solution)/shard_map/tab,tbf->taf/dot_general | solution.py:16
  109.3 8.6 %convolution_convert_fusion.3 = bf16[4,128,512]{2,0,1:T(4,128)(2,1)S(1)} fusion(f32[48,128,512]{2,0,1:T(8,128)} %copy.126, f32[48]{0:T(128)S(1)} %compare_convert_fusion, s32[48]{0:T(128)S(1)} %get-tuple-element.10), kind=kOutput, calls=%fused_computation.51 | convolution fusion | flops 151257472 | bytes 13107584 | tf_op jit(solution)/shard_map/rt,taf->raf/dot_general | solution.py:21
  119.4 60.9 %all-gather.11.cloned.1.call-done = bf16[1024,512]{1,0:T(8,128)(2,1)} async-done(((bf16[8,512]{1,0:T(8,128)(2,1)}), bf16[1024,512]{1,0:T(8,128)(2,1)}) %all-gather.11.cloned.1.call-update) | async-done | bytes 1048592 | tf_op jit(solution)/shard_map/all_gather | solution.py:102
  185.4 4.9 gather_fusion.5
  190.3 9.2 %convolution_bitcast_fusion.2 = f32[48,128,512]{1,2,0:T(8,128)} fusion(bf16[48,128,512]{2,1,0:T(8,128)(2,1)} %gather_fusion.5, bf16[1,48,128,128]{3,2,1,0:T(8,128)(2,1)S(1)} %copy-done), kind=kOutput, calls=%fused_computation.37 | convolution fusion | flops 805306368 | bytes 20447232 | tf_op jit(solution)/shard_map/tab,tbf->taf/dot_general | solution.py:16
  199.5 12.7 %copy.130 = f32[48,128,512]{2,0,1:T(8,128)} copy(f32[48,128,512]{1,2,0:T(8,128)} %convolution_bitcast_fusion.2) | data formatting | bytes 25165824 | tf_op jit(solution)/shard_map/tab,tbf->taf/dot_general | solution.py:16
  212.2 8.6 %convolution_convert_fusion.2 = bf16[4,128,512]{2,0,1:T(4,128)(2,1)S(1)} fusion(f32[48,128,512]{2,0,1:T(8,128)} %copy.130, f32[48]{0:T(128)S(1)} %compare_convert_fusion, s32[48]{0:T(128)S(1)} %get-tuple-element.10), kind=kOutput, calls=%fused_computation.50 | convolution fusion | flops 151257472 | bytes 13107584 | tf_op jit(solution)/shard_map/rt,taf->raf/dot_general | solution.py:21
  222.4 60.9 %all-gather.13.cloned.1.call-done = bf16[1024,512]{1,0:T(8,128)(2,1)} async-done(((bf16[8,512]{1,0:T(8,128)(2,1)}), bf16[1024,512]{1,0:T(8,128)(2,1)}) %all-gather.13.cloned.1.call-update) | async-done | bytes 1048592 | tf_op jit(solution)/shard_map/all_gather | solution.py:102
  288.6 4.9 gather_fusion.8
  293.4 9.2 %convolution_bitcast_fusion.1 = f32[48,128,512]{1,2,0:T(8,128)} fusion(bf16[48,128,512]{2,1,0:T(8,128)(2,1)} %gather_fusion.8, bf16[1,48,128,128]{3,2,1,0:T(8,128)(2,1)S(1)} %copy-done), kind=kOutput, calls=%fused_computation.36 | convolution fusion | flops 805306368 | bytes 20447232 | tf_op jit(solution)/shard_map/tab,tbf->taf/dot_general | solution.py:16
  302.6 12.7 %copy.134 = f32[48,128,512]{2,0,1:T(8,128)} copy(f32[48,128,512]{1,2,0:T(8,128)} %convolution_bitcast_fusion.1) | data formatting | bytes 25165824 | tf_op jit(solution)/shard_map/tab,tbf->taf/dot_general | solution.py:16
  315.4 8.6 %convolution_convert_fusion.1 = bf16[4,128,512]{2,0,1:T(4,128)(2,1)S(1)} fusion(f32[48,128,512]{2,0,1:T(8,128)} %copy.134, f32[48]{0:T(128)S(1)} %compare_convert_fusion, s32[48]{0:T(128)S(1)} %get-tuple-element.10), kind=kOutput, calls=%fused_computation.49 | convolution fusion | flops 151257472 | bytes 13107584 | tf_op jit(solution)/shard_map/rt,taf->raf/dot_general | solution.py:21
  333.6 52.8 %all-gather.15.cloned.1.call-done = bf16[1024,512]{1,0:T(8,128)(2,1)} async-done(((bf16[8,512]{1,0:T(8,128)(2,1)}), bf16[1024,512]{1,0:T(8,128)(2,1)}) %all-gather.15.cloned.1.call-update) | async-done | bytes 1048592 | tf_op jit(solution)/shard_map/all_gather | solution.py:102
  390.9 5.3 gather_fusion.11
  396.2 9.2 %convolution_bitcast_fusion = f32[48,128,512]{1,2,0:T(8,128)} fusion(bf16[48,128,512]{2,1,0:T(8,128)(2,1)} %gather_fusion.11, bf16[1,48,128,128]{3,2,1,0:T(8,128)(2,1)S(1)} %copy-done), kind=kOutput, calls=%fused_computation.35 | convolution fusion | flops 805306368 | bytes 20447232 | tf_op jit(solution)/shard_map/tab,tbf->taf/dot_general | solution.py:16
  405.4 12.7 %copy.138 = f32[48,128,512]{2,0,1:T(8,128)} copy(f32[48,128,512]{1,2,0:T(8,128)} %convolution_bitcast_fusion) | data formatting | bytes 25165824 | tf_op jit(solution)/shard_map/tab,tbf->taf/dot_general | solution.py:16
  418.1 8.7 %convolution_convert_fusion = bf16[4,128,512]{2,0,1:T(4,128)(2,1)S(1)} fusion(f32[48,128,512]{2,0,1:T(8,128)} %copy.138, f32[48]{0:T(128)S(1)} %compare_convert_fusion, s32[48]{0:T(128)S(1)} %get-tuple-element.10), kind=kOutput, calls=%fused_computation.48 | convolution fusion | flops 151257472 | bytes 13107584 | tf_op jit(solution)/shard_map/rt,taf->raf/dot_general | solution.py:21
  428.7 19.0 %stack.5 = bf16[512,5,512]{2,1,0:T(8,128)(2,1)} concatenate(bf16[512,1,512]{2,1,0:T(2,128)(2,1)S(1)} %copy-done.6, bf16[512,1,512]{2,1,0:T(2,128)(2,1)S(1)} %copy-done.7, bf16[512,1,512]{2,1,0:T(2,128)(2,1)} %copy.142, bf16[512,1,512]{2,1,0:T(2,128)(2,1)} %copy.143, bf16[512,1,512]{2,1,0:T(2,128)(2,1)} %copy.144), dimensions={1} | concatenate | bytes 5242880 | tf_op jit(solution)/shard_map/stack | solution.py:106
  447.7 5.1 gather_fusion.12
  452.9 7.1 all_to_all.17
  460.0 4.6 all-to-all-start.1
  466.8 38.6 %all-to-all-done.1 = bf16[16,32,2560]{2,1,0:T(8,128)(2,1)} async-done(((bf16[16,32,2560]{2,1,0:T(8,128)(2,1)}), bf16[16,32,2560]{2,1,0:T(8,128)(2,1)}, u32[]{:S(2)}, u32[]{:S(2)}) %all-to-all-start.1) | async-done | bytes 2621472 | tf_op jit(solution)/shard_map/all_to_all | solution.py:108
  505.4 5.9 reshape.312
  521.7 8.7 %mul.136 = f32[16,32,2560]{2,1,0:T(8,128)} reshape(f32[512,5,512]{2,1,0:T(8,128)} %mul.135) | data formatting | bytes 10485760 | tf_op jit(solution)/shard_map/mul | solution.py:28
  533.9 8.7 %sub.35 = f32[16,32,2560]{2,1,0:T(8,128)} reshape(f32[512,5,512]{2,1,0:T(8,128)} %sub.34) | data formatting | bytes 10485760 | tf_op jit(solution)/shard_map/sub | solution.py:26
  542.6 7.7 %multiply_convert_fusion.1 = bf16[16,32,2560]{2,1,0:T(8,128)(2,1)} fusion(f32[16,32,2560]{2,1,0:T(8,128)} %mul.136, f32[16,32,2560]{2,1,0:T(8,128)} %sub.35, f32[2560]{0:T(1024)S(1)} %mul.140, bf16[16,32,2560]{2,1,0:T(8,128)(2,1)} %all-to-all-done.1), kind=kLoop, calls=%fused_computation.31 | loop fusion | flops 6553600 | bytes 15738880 | tf_op jit(solution)/shard_map/convert_element_type | solution.py:37
  550.4 7.0 convert_element_type.147
  557.4 6.5 fusion.38
  563.9 15.1 %copy.151 = f32[512,5,8,64]{3,1,2,0:T(8,128)} copy(f32[512,5,8,64]{0,3,2,1:T(8,128)} %fusion.38) | data formatting | bytes 10485760 | tf_op jit(solution)/shard_map/dot_general | solution.py:38
  579.0 6.6 fusion.36
  585.6 14.9 %copy.152 = f32[512,5,8,64]{3,1,2,0:T(8,128)} copy(f32[512,5,8,64]{0,3,2,1:T(8,128)} %fusion.36) | data formatting | bytes 10485760 | tf_op jit(solution)/shard_map/dot_general | solution.py:41
  600.5 6.6 fusion.40
  607.1 14.9 %copy.153 = f32[512,5,8,64]{3,1,2,0:T(8,128)} copy(f32[512,5,8,64]{0,3,2,1:T(8,128)} %fusion.40) | data formatting | bytes 10485760 | tf_op jit(solution)/shard_map/dot_general | solution.py:44
  622.0 37.9 %fusion.2 = (f32[512,8,5]{2,1,0:T(8,128)S(1)}, f32[512,8,5,5]{2,3,1,0:T(8,128)}) fusion(f32[512,5,8,64]{3,1,2,0:T(8,128)} %copy.151, f32[512,5,8,64]{3,1,2,0:T(8,128)} %copy.152), kind=kOutput, calls=%fused_computation.17 | convolution fusion | flops 78827520 | bytes 10977280 | tf_op jit(solution)/shard_map/nihd,njhd->nhij/dot_general | solution.py:47
  659.9 38.8 %convert_bitcast_fusion = bf16[512,5,8,64]{3,1,2,0:T(8,128)(2,1)S(1)} fusion(f32[512,5,8,64]{3,1,2,0:T(8,128)} %copy.153, f32[512,8,5,5]{2,3,1,0:T(8,128)} %get-tuple-element.13, f32[512,8,5]{2,1,0:T(8,128)S(1)} %get-tuple-element.12), kind=kOutput, calls=%fused_computation.26 | convolution fusion | flops 80158720 | bytes 8355840 | tf_op jit(solution)/shard_map/nhij,njhd->nihd/dot_general | solution.py:52
  702.3 7.9 %convert_element_type.150 = bf16[2560,512]{1,0:T(8,128)(2,1)} reshape(bf16[512,5,8,64]{3,2,1,0:T(8,128)(2,1)} %copy.155) | data formatting | bytes 5242880 | tf_op jit(solution)/shard_map/convert_element_type | solution.py:53
  710.2 5.1 fusion.83
  718.7 12.7 %convolution_add_fusion.1 = f32[2560,512]{1,0:T(8,128)} fusion(f32[2560,512]{1,0:T(8,128)} %copy-done.2, f32[512]{0:T(512)S(1)} %bitcast.168, f32[2560]{0:T(1024)S(1)} %add_rsqrt_fusion, f32[2560]{0:T(1024)S(1)} %broadcast_multiply_fusion, bf16[1,1024,512]{2,1,0:T(8,128)(2,1)S(1)} %copy-done.12, bf16[1,512,1024]{2,1,0:T(8,128)(2,1)S(1)} %copy-done.13), kind=kOutput, calls=%fused_computation.34 | convolution fusion | flops 5398855680 | bytes 12605440 | tf_op jit(solution)/shard_map/dot_general | solution.py:59
  731.5 7.5 reshape.311
  739.0 4.5 slice.81
  743.5 4.4 slice.80
  747.9 4.3 fusion.15
  753.7 10.9 %fusion.79 = f32[512,1,512]{2,1,0:T(1,128)S(1)} fusion(f32[512,4,1]{1,2,0:T(1,128)S(1)} %copy.166, f32[512,5,512]{2,1,0:T(8,128)} %reshape.311), kind=kOutput, calls=%fused_computation.126 | convolution fusion | flops 12582912 | bytes 5251072 | tf_op jit(solution)/shard_map/nk,nkf->nf/dot_general | solution.py:69
  (98 shorter events, 66.9 us)
Async XLA Ops:
  6.5 80.8 %copy-start = (bf16[1,48,128,128]{3,2,1,0:T(8,128)(2,1)S(1)}, bf16[1,48,128,128]{3,2,1,0:T(8,128)(2,1)}, u32[]{:S(2)}) copy-start(bf16[1,48,128,128]{3,2,1,0:T(8,128)(2,1)} %param.13) | copy-start | bytes 4718596
  6.5 74.8 %copy-start.8 = (bf16[512,512]{1,0:T(8,128)(2,1)S(1)}, bf16[512,512]{1,0:T(8,128)(2,1)}, u32[]{:S(2)}) copy-start(bf16[512,512]{1,0:T(8,128)(2,1)} %param.12) | copy-start | bytes 1572868
  6.5 70.8 %all-gather.9.cloned.1.call-start = ((), (), s32[]{:S(2)}) async-start(), calls=%async_computation.2 | async-start | bytes 1056768 | tf_op jit(solution)/shard_map/all_gather | solution.py:102
  11.1 21.0 %all-to-all-start = ((s32[128,1,4]{2,1,0:T(1,128)}), s32[128,1,4]{2,1,0:T(1,128)S(1)}, u32[]{:S(2)}, u32[]{:S(2)}) async-start(s32[128,1,4]{2,1,0:T(1,128)} %bitcast.7), calls=%async_computation | async-start | bytes 131072 | tf_op jit(solution)/shard_map/all_to_all | solution.py:94
  22.6 157.7 %all-gather.11.cloned.1.call-start = ((), (), s32[]{:S(2)}) async-start(), calls=%async_computation.3 | async-start | bytes 1056768 | tf_op jit(solution)/shard_map/all_gather | solution.py:102
  119.2 164.1 %all-gather.13.cloned.1.call-start = ((), (), s32[]{:S(2)}) async-start(), calls=%async_computation.4 | async-start | bytes 1056768 | tf_op jit(solution)/shard_map/all_gather | solution.py:102
  220.9 62.4 %copy-start.3 = (bf16[4,128,512]{2,1,0:T(8,128)(2,1)}, bf16[4,128,512]{2,1,0:T(8,128)(2,1)S(1)}, u32[]{:S(2)}) copy-start(bf16[4,128,512]{2,1,0:T(8,128)(2,1)S(1)} %copy.131) | copy-start | bytes 1572868
  222.1 164.3 %all-gather.15.cloned.1.call-start = ((), (), s32[]{:S(2)}) async-start(), calls=%async_computation.5 | async-start | bytes 1056768 | tf_op jit(solution)/shard_map/all_gather | solution.py:102
  315.3 12.8 %copy-start.11 = (s32[1,512]{1,0:T(1,128)S(1)}, s32[1,512]{1,0:T(1,128)}, u32[]{:S(2)}) copy-start(s32[1,512]{1,0:T(1,128)} %param.18) | copy-start | bytes 6148
  315.4 14.6 %copy-start.4 = (bf16[4,128,512]{2,1,0:T(8,128)(2,1)S(1)}, bf16[4,128,512]{2,1,0:T(8,128)(2,1)}, u32[]{:S(2)}) copy-start(bf16[4,128,512]{2,1,0:T(8,128)(2,1)} %copy-done.3) | copy-start | bytes 1572868
  324.1 62.4 %copy-start.5 = (bf16[4,128,512]{2,1,0:T(8,128)(2,1)}, bf16[4,128,512]{2,1,0:T(8,128)(2,1)S(1)}, u32[]{:S(2)}) copy-start(bf16[4,128,512]{2,1,0:T(8,128)(2,1)S(1)} %copy.135) | copy-start | bytes 1572868
  418.1 10.6 %copy-start.6 = (bf16[512,1,512]{2,1,0:T(2,128)(2,1)S(1)}, bf16[512,1,512]{2,1,0:T(2,128)(2,1)}, u32[]{:S(2)}) copy-start(bf16[512,1,512]{2,1,0:T(2,128)(2,1)} %copy.140) | copy-start | bytes 1572868
  418.1 10.6 %copy-start.7 = (bf16[512,1,512]{2,1,0:T(2,128)(2,1)S(1)}, bf16[512,1,512]{2,1,0:T(2,128)(2,1)}, u32[]{:S(2)}) copy-start(bf16[512,1,512]{2,1,0:T(2,128)(2,1)} %copy.141) | copy-start | bytes 1572868
  452.9 11.8 %copy-start.10 = (f32[1,2,512]{2,1,0:T(2,128)S(1)}, f32[1,2,512]{2,1,0:T(2,128)}, u32[]{:S(2)}) copy-start(f32[1,2,512]{2,1,0:T(2,128)} %param.22) | copy-start | bytes 12292
  460.0 45.4 %all-to-all-start.1 = ((bf16[16,32,2560]{2,1,0:T(8,128)(2,1)}), bf16[16,32,2560]{2,1,0:T(8,128)(2,1)}, u32[]{:S(2)}, u32[]{:S(2)}) async-start(bf16[16,32,2560]{2,1,0:T(8,128)(2,1)} %all_to_all.17), calls=%async_computation.1 | async-start | bytes 5242880 | tf_op jit(solution)/shard_map/all_to_all | solution.py:108
  715.2 2.5 copy-start.2
  715.2 3.5 copy-start.12
  715.2 3.5 copy-start.13
  739.0 8.9 %copy-start.9 = (f32[2,512]{1,0:T(2,128)S(1)}, f32[2,512]{1,0:T(2,128)}, u32[]{:S(2)}) copy-start(f32[2,512]{1,0:T(2,128)} %param.23) | copy-start | bytes 12292
  753.6 12.1 %copy-start.1 = (bf16[1,48,128,128]{3,2,1,0:T(8,128)(2,1)S(1)}, bf16[1,48,128,128]{3,2,1,0:T(8,128)(2,1)}, u32[]{:S(2)}) copy-start(bf16[1,48,128,128]{3,2,1,0:T(8,128)(2,1)} %param.13) | copy-start | bytes 4718596
Sparse Core Ops, SparseCore 0:
  10.1 67.1 all-gather.8
  119.3 60.9 all-gather.10
  222.2 60.9 all-gather.12
  325.4 60.9 all-gather.14
where the time goes:
time: 784 us; the launch traced here: 772 us
  waiting for transfers between devices  265 us (34%)
  local copies, waits for them, and re-layouts  252 us (32%)
  matrix products  202 us (26%)
  other arithmetic  23 us (3%)
  starting transfers between devices  16.6 us (2%)
  between operations  14.5 us (2%)
    all_gather x4, waiting for transfers between devices, local(): table = lax.all_gather(edge_rows, ('dom', 'shard'), axis=0, tiled=True)  218 us
    dot_general x4, local copies, waits for them, and re-layouts, propagate(): jnp.einsum('tab,tbf->taf', tile_set, picked, preferred_element_type=jnp.f...  51 us
    dot_general x1, matrix products, encode(): jnp.einsum('nhij,njhd->nihd', weights, value_vecs, precision=lax.Precisio...  38.8 us
    all_to_all x1, waiting for transfers between devices, local(): lax.all_to_all(flat_rows, 'shard', split_axis=0, concat_axis=0, tiled=True)  38.6 us
    dot_general x1, matrix products, encode(): jnp.einsum('nihd,njhd->nhij', queries, key_vecs, precision=lax.Precision....  37.9 us
    dot_general x4, matrix products, propagate(): jnp.einsum('tab,tbf->taf', tile_set, picked, preferred_element_type=jnp.f...  36.7 us
    dot_general x4, matrix products, propagate(): jnp.einsum('rt,taf->raf', selector, product, precision=lax.Precision.HIGH...  34.5 us
    another operation x2, local copies, waits for them, and re-layouts, local(): stacked = jnp.stack(hop_list, 1)[row_order]  21.8 us
  transfers between devices with their start and end apart: 6, of which 6 were waited for; matrix products, arithmetic and copies ran while one was open for 2% of the time, Pallas kernels for 0%

commit v1 on v0

v1 whole, which is shorter than its diff:
```python
import functools

import jax
import jax.numpy as jnp
from jax import lax
from jax.experimental import pallas as pl
from jax.experimental.pallas import tpu as pltpu
from jax.sharding import PartitionSpec as P

F32, BF16, I32 = jnp.float32, jnp.bfloat16, jnp.int32
MESH = pl.DeviceIdType.MESH
HEADS = 8
HOPS = 4
TOKENS = HOPS + 1
LANES = 128
PARTS = 4
BLOCK = 16
CHUNK = 128
SUB = 32


def dot(a, b):
    return jnp.dot(a, b, preferred_element_type=F32)


def iota(shape, dim):
    return lax.broadcasted_iota(I32, shape, dim)


def onehot(hit):
    return jnp.where(hit, 1.0, 0.0).astype(BF16)


def layer_norm(x, gain):
    center = x - jnp.mean(x, -1, keepdims=True)
    spread = jnp.mean(center * center, -1, keepdims=True)
    return center * lax.rsqrt(spread + 1e-05) * gain


def build_adjacency(coords, count, tiles, out, total):
    size = tiles.shape[2]
    rows, cols = out.shape[0] // size, out.shape[1] // size
    for r in range(rows):
        for c in range(cols):
            total[r, c] = jnp.zeros((size, size), F32)

    def step(t, carry):
        r, c = coords[0, t, 0], coords[0, t, 1]
        total[r, c] += tiles[0, t].astype(F32)
        return carry

    lax.fori_loop(0, count[0], step, 0)
    for r in range(rows):
        for c in range(cols):
            out[r * size : (r + 1) * size, c * size : (c + 1) * size] = total[r, c].astype(BF16)


def window(
    feat,
    adj,
    border,
    picks,
    order,
    attn_any,
    fin_any,
    fout_any,
    gain,
    readw,
    out,
    hops,
    send,
    recv,
    psend,
    own_edge,
    halo_edge,
    adj_own,
    adj_halo,
    halo,
    own,
    q,
    k,
    v,
    attn,
    fin,
    fout,
    pair,
    score,
    ctx,
    hid,
    mid,
    stage,
    send_sem,
    recv_sem,
    weight_sem,
    out_send_sem,
    out_recv_sem,
):
    n_dom, n_shard = lax.axis_size("dom"), lax.axis_size("shard")
    n = n_dom * n_shard
    dom, shard = lax.axis_index("dom"), lax.axis_index("shard")
    me = dom * n_shard + shard
    rows, width = feat.shape

    barrier = pltpu.get_barrier_semaphore()

    def greet(i, carry):
        p = lax.rem(me + i, n)
        pl.semaphore_signal(
            barrier, inc=1, device_id=(p // n_shard, lax.rem(p, n_shard)), device_id_type=MESH
        )
        return carry

    lax.fori_loop(1, n, greet, 0)
    loads = [
        pltpu.make_async_copy(attn_any, attn, weight_sem.at[0]),
        pltpu.make_async_copy(fin_any, fin, weight_sem.at[1]),
        pltpu.make_async_copy(fout_any, fout, weight_sem.at[2]),
    ]
    for load in loads:
        load.start()

    n_pick = picks.shape[2]
    n_edge = border.shape[1]
    pickf = picks[0].astype(F32).astype(BF16)
    lane = iota((n_pick, LANES), 1)
    spread = onehot(lax.rem(lane // n_edge, n_pick) == iota((n_pick, LANES), 0))
    chosen = dot(pickf, spread).astype(I32)
    chosen = onehot(chosen == lax.rem(iota((n, LANES), 1), n_edge))
    for g in range(n * BLOCK // 256):
        shape = (256, n)
        repeat = onehot(iota(shape, 0) // BLOCK + g * (256 // BLOCK) == iota(shape, 1))
        shape = (256, LANES)
        keep = iota(shape, 1) // n_edge == lax.rem(iota(shape, 0), BLOCK)
        psend[g * 256 : (g + 1) * 256, :] = jnp.where(keep, dot(repeat, chosen), 0.0).astype(BF16)

    def edge_of(index_rows):
        at = jnp.zeros((n_edge, rows), I32)
        for b in range(n_edge):
            at = jnp.where(iota((n_edge, rows), 0) == b, border[0, b], at)
        hit = jnp.where(at == index_rows, 1.0, 0.0)
        return jnp.concatenate([hit] * (LANES // n_edge), 0).astype(BF16)

    def diagonal(x):
        step = LANES // PARTS
        return jnp.concatenate(
            [x[c * step : (c + 1) * step, c * LANES : (c + 1) * LANES] for c in range(PARTS)], 0
        )

    def post(r, edge):
        edge = edge.astype(BF16)
        for g in range(n * BLOCK // 256):
            send[r, g * 256 : (g + 1) * 256, :] = dot(psend[g * 256 : (g + 1) * 256, :], edge).astype(BF16)

        def one(i, carry):
            p = lax.rem(me + i * 37, n)
            pltpu.make_async_remote_copy(
                src_ref=send.at[r, pl.ds(pl.multiple_of(p * BLOCK, BLOCK), BLOCK)],
                dst_ref=recv.at[r, pl.ds(pl.multiple_of(me * BLOCK, BLOCK), BLOCK)],
                send_sem=send_sem.at[r],
                recv_sem=recv_sem.at[r],
                device_id=(p // n_shard, lax.rem(p, n_shard)),
                device_id_type=MESH,
            ).start()
            return carry

        lax.fori_loop(1, n, one, 0)
        mine = pl.ds(pl.multiple_of(me * BLOCK, BLOCK), BLOCK)
        pltpu.make_async_copy(send.at[r, mine], recv.at[r, mine], recv_sem.at[r]).start()

    first = diagonal(dot(edge_of(iota((n_edge, rows), 1)), feat[...]))
    pl.semaphore_wait(barrier, n - 1)
    post(0, first)

    place_t = onehot(iota((rows, rows), 0) == order[...])
    place = place_t.astype(F32).T.astype(BF16)
    hops[0] = dot(place, feat[...]).astype(BF16)
    adj_own[...] = dot(dot(place, adj[:, :rows]).astype(BF16), place_t).astype(BF16)
    adj_halo[...] = dot(place, adj[:, rows:]).astype(BF16)
    edge = edge_of(order[...])
    own_edge[...] = dot(edge, adj_own[...]).astype(BF16)
    halo_part = dot(edge, adj_halo[...]).astype(BF16)
    group = LANES // n_pick
    shape = (LANES, LANES * PARTS)
    widen = onehot(
        (iota(shape, 0) // n_pick == iota(shape, 1) // BLOCK)
        & (lax.rem(iota(shape, 0), n_pick) == lax.rem(iota(shape, 1), n_pick))
    )
    shape = (LANES, LANES * PARTS)
    same = iota(shape, 0) // (LANES // PARTS) == lax.rem(iota(shape, 1) // n_pick, PARTS)
    for g in range(n // group):
        wide = dot(halo_part[:, g * LANES : (g + 1) * LANES], widen)
        halo_edge[:, g * LANES * PARTS : (g + 1) * LANES * PARTS] = jnp.where(same, wide, 0.0).astype(BF16)

    def source(i):
        head = lax.rem(i // (LANES // HEADS), HEADS)
        return head * (width // HEADS) + (i // LANES) * (LANES // HEADS) + lax.rem(i, LANES // HEADS)

    shape = (width, width)
    by_row = onehot(iota(shape, 1) == source(iota(shape, 0)))
    by_col = onehot(iota(shape, 0) == source(iota(shape, 1)))
    loads[0].wait()
    for i in range(3):
        attn[0, i] = dot(attn[0, i], by_col).astype(BF16)
    attn[0, 3] = dot(by_row, attn[0, 3]).astype(BF16)

    per = 256 // BLOCK
    shape = (256, 256)
    row, col = iota(shape, 0), iota(shape, 1)
    regroup = onehot(
        (lax.rem(row // n_pick, per) == col // BLOCK)
        & (row // (256 // PARTS) == lax.rem(col // n_pick, PARTS))
        & (lax.rem(row, n_pick) == lax.rem(col, n_pick))
    )

    def project(h):
        def part(b, carry):
            at = pl.ds(pl.multiple_of(b * 256, 256), 256)
            a = layer_norm(hops[h, at, :].astype(F32), gain[0, 0:1, :]).astype(BF16)
            q[h, at, :] = dot(a, attn[0, 0])
            k[h, at, :] = dot(a, attn[0, 1])
            v[h, at, :] = dot(a, attn[0, 2])
            return carry

        lax.fori_loop(0, rows // 256, part, 0)

    def hop(r, carry):
        x = hops[r]
        own_part = diagonal(dot(own_edge[...], x))
        own[...] = dot(adj_own[...], x)
        project(r)
        pltpu.make_async_copy(recv.at[r], recv.at[r], recv_sem.at[r]).wait()

        @pl.when(r < HOPS - 1)
        def _():
            post(r + 1, own_part + dot(halo_edge[...], recv[r]))

        span = 256 // PARTS
        for g in range(n * BLOCK // 512):
            both = jnp.concatenate(
                [recv[r, g * 512 : g * 512 + 256, :], recv[r, g * 512 + 256 : (g + 1) * 512, :]], 1
            )
            moved = dot(regroup, both).astype(BF16)
            for c in range(PARTS):
                for d in range(2):
                    halo[(2 * g + d) * span : (2 * g + d + 1) * span, c * LANES : (c + 1) * LANES] = moved[
                        c * span : (c + 1) * span, d * LANES : (d + 1) * LANES
                    ]
        hops[r + 1] = (own[...] + dot(adj_halo[...], halo[...])).astype(BF16)
        return carry

    lax.fori_loop(0, HOPS, hop, 0)
    project(HOPS)
    loads[1].wait()
    loads[2].wait()

    shape = (2 * LANES, LANES)
    seg = LANES // HEADS
    gather = jnp.where(
        lax.rem(iota(shape, 0), LANES) // seg == iota(shape, 1) // seg, (width // HEADS) ** -0.5, 0.0
    ).astype(BF16)
    share = rows // n_shard
    n_chunk = rows // CHUNK

    def lanes(c):
        return slice(c * LANES, (c + 1) * LANES)

    def layer(step, carry):
        at_chunk = lax.rem(step + shard // (n_shard // n_chunk), n_chunk)
        base = at_chunk * CHUNK

        def scores(b, carry):
            at = pl.ds(pl.multiple_of(base + b * SUB, SUB), SUB)
            for i in range(TOKENS):
                qs = [q[i, at, lanes(c)] for c in range(PARTS)]
                for j in range(TOKENS):
                    s = qs[0] * k[j, at, lanes(0)]
                    for c in range(1, PARTS):
                        s += qs[c] * k[j, at, lanes(c)]
                    high = s.astype(BF16)
                    low = (s - high.astype(F32)).astype(BF16)
                    to = pl.ds(pl.multiple_of((i * TOKENS + j) * CHUNK + b * SUB, SUB), SUB)
                    pair[to, lanes(0)] = high
                    pair[to, lanes(1)] = low
            return carry

        lax.fori_loop(0, CHUNK // SUB, scores, 0)
        score[...] = dot(pair[...], gather)

        def mix(b, carry):
            at = pl.ds(pl.multiple_of(base + b * SUB, SUB), SUB)
            for i in range(TOKENS):
                s = [
                    score[pl.ds(pl.multiple_of((i * TOKENS + j) * CHUNK + b * SUB, SUB), SUB), :]
                    for j in range(TOKENS)
                ]
                top = functools.reduce(jnp.maximum, s)
                e = [jnp.exp(x - top) for x in s]
                scale = 1.0 / functools.reduce(jnp.add, e)
                w = [x * scale for x in e]
                to = pl.ds(pl.multiple_of(i * CHUNK + b * SUB, SUB), SUB)
                for c in range(PARTS):
                    total = w[0] * v[0, at, lanes(c)]
                    for j in range(1, TOKENS):
                        total += w[j] * v[j, at, lanes(c)]
                    ctx[to, lanes(c)] = total.astype(BF16)
            return carry

        lax.fori_loop(0, CHUNK // SUB, mix, 0)
        at = pl.ds(pl.multiple_of(base, CHUNK), CHUNK)
        hid[...] = dot(ctx[...], attn[0, 3])
        for i in range(TOKENS):
            to = slice(i * CHUNK, (i + 1) * CHUNK)
            h = hops[i, at, :].astype(F32) + hid[to, :]
            hid[to, :] = h
            ctx[to, :] = layer_norm(h, gain[0, 1:2, :]).astype(BF16)
        for b in range(mid.shape[1] // 256):
            x = dot(ctx[...], fin[0, :, b * 256 : (b + 1) * 256])
            mid[:, b * 256 : (b + 1) * 256] = jax.nn.gelu(x, approximate=True).astype(BF16)
        hid[...] += dot(mid[...], fout[0])

        z0 = hid[0:CHUNK, :]
        base_score = jnp.sum(z0 * readw[0:1, :], -1, keepdims=True)
        s = [
            base_score + jnp.sum(hid[i * CHUNK : (i + 1) * CHUNK, :] * readw[1:2, :], -1, keepdims=True)
            for i in range(1, TOKENS)
        ]
        top = functools.reduce(jnp.maximum, s)
        e = [jnp.exp(x - top) for x in s]
        scale = 1.0 / functools.reduce(jnp.add, e)
        state = z0
        for i in range(1, TOKENS):
            state += (e[i - 1] * scale) * hid[i * CHUNK : (i + 1) * CHUNK, :]
        stage[at, :] = state.astype(BF16)

        def deal(t, carry):
            to = at_chunk * (CHUNK // share) + t
            src = stage.at[pl.ds(pl.multiple_of(to * share, share), share)]
            dst = out.at[pl.ds(pl.multiple_of(shard * share, share), share)]

            @pl.when(to != shard)
            def _():
                pltpu.make_async_remote_copy(
                    src_ref=src,
                    dst_ref=dst,
                    send_sem=out_send_sem,
                    recv_sem=out_recv_sem,
                    device_id=(dom, to),
                    device_id_type=MESH,
                ).start()

            @pl.when(to == shard)
            def _():
                pltpu.make_async_copy(src, dst, out_recv_sem).start()

            return carry

        lax.fori_loop(0, CHUNK // share, deal, 0)
        return carry

    lax.fori_loop(0, n_chunk, layer, 0)

    sent = send.at[0, pl.ds(0, (n - 1) * BLOCK)]
    for r in range(HOPS):
        pltpu.make_async_copy(sent, sent, send_sem.at[r]).wait()
    sent = stage.at[pl.ds(0, rows - share)]
    pltpu.make_async_copy(sent, sent, out_send_sem).wait()
    pltpu.make_async_copy(out, out, out_recv_sem).wait()


def local(
    features,
    tile_values,
    tile_coords,
    tile_count,
    boundary_index,
    peer_pick,
    shuffle_order,
    attn_weight,
    ffn_in,
    ffn_out,
    norm_gain,
    read_weight,
):
    rows, width = features.shape
    size = tile_values.shape[2]
    n, n_pick = peer_pick.shape[1], peer_pick.shape[2]
    halo_rows = n * n_pick
    hidden = ffn_in.shape[2]
    vmem = pl.BlockSpec(memory_space=pltpu.VMEM)
    smem = pl.BlockSpec(memory_space=pltpu.SMEM)
    hbm = pl.BlockSpec(memory_space=pl.ANY)
    adj = pl.pallas_call(
        build_adjacency,
        out_shape=jax.ShapeDtypeStruct((rows, rows + halo_rows), BF16),
        in_specs=[smem, smem, vmem],
        out_specs=vmem,
        scratch_shapes=[pltpu.VMEM((8, 8, size, size), F32)],
        compiler_params=pltpu.CompilerParams(vmem_limit_bytes=24 * 2**20),
        name="adjacency",
    )(tile_coords, tile_count, tile_values)
    message = n * BLOCK
    return pl.pallas_call(
        window,
        out_shape=jax.ShapeDtypeStruct((rows, width), BF16),
        in_specs=[vmem, vmem, smem, vmem, vmem, hbm, hbm, hbm, vmem, vmem],
        out_specs=vmem,
        scratch_shapes=[
            pltpu.VMEM((TOKENS, rows, width), BF16),
            pltpu.VMEM((HOPS, message, LANES), BF16),
            pltpu.VMEM((HOPS, message, LANES), BF16),
            pltpu.VMEM((message, LANES), BF16),
            pltpu.VMEM((LANES, rows), BF16),
            pltpu.VMEM((LANES, message), BF16),
            pltpu.VMEM((rows, rows), BF16),
            pltpu.VMEM((rows, halo_rows), BF16),
            pltpu.VMEM((halo_rows, width), BF16),
            pltpu.VMEM((rows, width), F32),
            pltpu.VMEM((TOKENS, rows, width), F32),
            pltpu.VMEM((TOKENS, rows, width), F32),
            pltpu.VMEM((TOKENS, rows, width), F32),
            pltpu.VMEM(attn_weight.shape, BF16),
            pltpu.VMEM(ffn_in.shape, BF16),
            pltpu.VMEM(ffn_out.shape, BF16),
            pltpu.VMEM((TOKENS * TOKENS * CHUNK, 2 * LANES), BF16),
            pltpu.VMEM((TOKENS * TOKENS * CHUNK, LANES), F32),
            pltpu.VMEM((TOKENS * CHUNK, width), BF16),
            pltpu.VMEM((TOKENS * CHUNK, width), F32),
            pltpu.VMEM((TOKENS * CHUNK, hidden), BF16),
            pltpu.VMEM((rows, width), BF16),
            pltpu.SemaphoreType.DMA((HOPS,)),
            pltpu.SemaphoreType.DMA((HOPS,)),
            pltpu.SemaphoreType.DMA((3,)),
            pltpu.SemaphoreType.DMA,
            pltpu.SemaphoreType.DMA,
        ],
        compiler_params=pltpu.CompilerParams(
            collective_id=0, has_side_effects=True, vmem_limit_bytes=56 * 2**20
        ),
        name="window",
    )(
        features,
        adj,
        boundary_index,
        peer_pick,
        shuffle_order,
        attn_weight,
        ffn_in,
        ffn_out,
        norm_gain,
        read_weight,
    )


def solution(mesh):
    placed = (
        P(("dom", "shard"), None),
        P(("dom", "shard"), None, None, None),
        P(("dom", "shard"), None, None),
        P(("dom", "shard")),
        P(("dom", "shard"), None),
        P(("dom", "shard"), None, None),
        P(("dom", "shard"), None),
        P(),
        P(),
        P(),
        P(),
        P(),
    )
    return jax.shard_map(
        local, mesh=mesh, in_specs=placed, out_specs=P(("dom", "shard"), None), check_vma=False
    )
```

time: 784 us -> 93.8 us (0.12); the launches traced: 772 us -> 93.5 us
  waiting for transfers between devices: 265 us -> 0 us
  local copies, waits for them, and re-layouts: 252 us -> 6.43 us
  matrix products: 202 us -> 0 us
  Pallas kernels: 0 us -> 86.4 us
  other arithmetic: 23 us -> 0 us
  starting transfers between devices: 16.6 us -> 0 us
  between operations: 14.5 us -> 0.68 us
    all_gather x4 -> x0, waiting for transfers between devices: 218 us -> none  [local(): table = lax.all_gather(edge_rows, ('dom', 'shard'), axis=0, tiled=True)]
    dot_general x18 -> x0, matrix products: 202 us -> none  [the longest x1 38.8 us: encode(): jnp.einsum('nhij,njhd->nihd', weights, value_vecs, precision=lax.Precisio...]
    dot_general x8 -> x0, local copies, waits for them, and re-layouts: 96.1 us -> none  [the longest x4 51 us: propagate(): jnp.einsum('tab,tbf->taf', tile_set, picked, preferred_element_type=jnp.f...]
    pallas_call x0 -> x2, Pallas kernels: none -> 86.4 us  [the longest x1 85 us: local(): pl.pallas_call(window, out_shape=jax.ShapeDtypeStruct((rows, width), BF16...]
    all_to_all x2 -> x0, waiting for transfers between devices: 46.5 us -> none  [the longest x1 38.6 us: local(): lax.all_to_all(flat_rows, 'shard', split_axis=0, concat_axis=0, tiled=True)]
    gather x13 -> x0, local copies, waits for them, and re-layouts: 46.2 us -> none  [the longest x4 19.9 us: propagate(): picked = sources[tile_place[:, 1]]]
    convert_element_type x12 -> x0, local copies, waits for them, and re-layouts: 32.1 us -> none  [the longest x2 11.5 us: encode(): context.reshape(node_count * token_count, feat_width).astype(jnp.bfloat16)]
    another operation x2 -> x0, local copies, waits for them, and re-layouts: 21.8 us -> none  [local(): stacked = jnp.stack(hop_list, 1)[row_order]]
  transfers between devices with their start and end apart: 6 -> 0, of which waited for: 6 -> 0; matrix products, arithmetic and copies ran while one was open for 2% -> 0% of each run, Pallas kernels for 0% -> 0%
where the time goes in v1:
time: 93.8 us; the launch traced here: 93.5 us
  Pallas kernels  86.4 us (92%)
  local copies, waits for them, and re-layouts  6.43 us (7%)
    pallas_call x1, Pallas kernels, local(): pl.pallas_call(window, out_shape=jax.ShapeDtypeStruct((rows, width), BF16...  85 us
    unnamed x7, local copies, waits for them, and re-layouts  6.43 us

profile of v1, /device:TPU:1, one launch (start us, length us, event | category | flops | bytes accessed | tf_op | source)
XLA Modules:
  0.0 93.5 jit_solution(11674555105754886743)
XLA Ops:
  0.7 0.8 copy.13.coords
  1.4 1.4 %copy.14.picks = s32[1,128,4]{2,1,0:T(8,128)} copy(s32[1,128,4]{1,2,0:T(4,128)} %param.17) | data formatting | bytes 4096 | tf_op args[5]
  2.8 0.0 copy-start.1
  2.8 1.4 %copy-done.1 = bf16[1,48,128,128]{3,2,1,0:T(8,128)(2,1)S(1)} copy-done((bf16[1,48,128,128]{3,2,1,0:T(8,128)(2,1)S(1)}, bf16[1,48,128,128]{3,2,1,0:T(8,128)(2,1)}, u32[]{:S(2)}) %copy-start.1) | copy-done | bytes 1572888
  4.2 1.4 %adjacency.1.adj = bf16[512,1024]{1,0:T(8,128)(2,1)S(1)} custom-call(s32[1,48,2]{2,1,0:T(8,128)S(1)} %copy.13.coords, s32[1]{0:T(128)S(6)} %copy.16.count, bf16[1,48,128,128]{3,2,1,0:T(8,128)(2,1)S(1)} %copy-done.1), custom_call_target="tpu_custom_call" | custom-call | tf_op jit(solution)/shard_map/adjacency/pallas_call | solution.py:392
  5.7 0.0 copy-start
  5.7 1.0 %copy-done = bf16[512,1024]{1,0:T(8,128)(2,1)} copy-done((bf16[512,1024]{1,0:T(8,128)(2,1)}, bf16[512,1024]{1,0:T(8,128)(2,1)S(1)}, u32[]{:S(2)}) %copy-start) | copy-done | bytes 1048600
  6.7 85.0 %window.1 = bf16[512,512]{1,0:T(8,128)(2,1)} custom-call(bf16[512,512]{1,0:T(8,128)(2,1)} %feat.1, bf16[512,1024]{1,0:T(8,128)(2,1)} %copy-done, s32[1,8]{1,0:T(1,128)} %border.1, s32[1,128,4]{2,1,0:T(8,128)} %copy.14.picks, s32[1,512]{1,0:T(1,128)} %order.1, bf16[1,4,512,512]{3,2,1,0:T(8,128)(2,1)} %attn_any.1, bf16[1,512,1024]{2,1,0:T(8,128)(2,1)} %fin_any.1, ...), custom_call_target="tpu_custom_call" | custom-call | tf_op jit(solution)/shard_map/window/pallas_call | solution.py:402
  91.6 1.9 %copy.17 = bf16[512,512]{1,0:T(8,128)(2,1)} copy(bf16[512,512]{1,0:T(8,128)(2,1)} %window.1) | data formatting | bytes 1048576
Async XLA Ops:
  2.8 1.4 %copy-start.1 = (bf16[1,48,128,128]{3,2,1,0:T(8,128)(2,1)S(1)}, bf16[1,48,128,128]{3,2,1,0:T(8,128)(2,1)}, u32[]{:S(2)}) copy-start(bf16[1,48,128,128]{3,2,1,0:T(8,128)(2,1)} %tiles.1) | copy-start | bytes 4718596
  5.7 1.0 %copy-start = (bf16[512,1024]{1,0:T(8,128)(2,1)}, bf16[512,1024]{1,0:T(8,128)(2,1)S(1)}, u32[]{:S(2)}) copy-start(bf16[512,1024]{1,0:T(8,128)(2,1)S(1)} %adjacency.1.adj) | copy-start | bytes 3145732

commit v2 on v1

v2 whole, which is shorter than its diff:
```python
import functools

import jax
import jax.numpy as jnp
from jax import lax
from jax.experimental import pallas as pl
from jax.experimental.pallas import tpu as pltpu
from jax.sharding import PartitionSpec as P

F32, BF16, I32 = jnp.float32, jnp.bfloat16, jnp.int32
MESH = pl.DeviceIdType.MESH
SIDE = 4
HEADS = 8
HOPS = 4
TOKENS = HOPS + 1
LANES = 128
PARTS = 4
HALVES = 2
EACH = PARTS // HALVES
BLOCK = 8
CHUNK = 128
SUB = 32


def dot(a, b):
    return jnp.dot(a, b, preferred_element_type=F32)


def iota(shape, dim):
    return lax.broadcasted_iota(I32, shape, dim)


def onehot(hit):
    return jnp.where(hit, 1.0, 0.0).astype(BF16)


def layer_norm(x, gain):
    center = x - jnp.mean(x, -1, keepdims=True)
    spread = jnp.mean(center * center, -1, keepdims=True)
    return center * lax.rsqrt(spread + 1e-05) * gain


def window(
    feat,
    coords,
    count,
    border,
    picks,
    order,
    tiles_any,
    attn_any,
    fin_any,
    fout_any,
    gain,
    readw,
    out,
    hops,
    send,
    recv,
    psend,
    own_edge,
    halo_edge,
    adj_own,
    adj_halo,
    halo,
    own,
    own_diag,
    q,
    k,
    v,
    attn,
    fin,
    fout,
    tiles,
    total,
    link,
    link_at,
    adj,
    score,
    ctx,
    norm,
    hid,
    mid,
    stage,
    send_sem,
    recv_sem,
    load_sem,
    link_sem,
    out_send_sem,
    out_recv_sem,
):
    n_dom, n_shard = lax.axis_size("dom"), lax.axis_size("shard")
    n = n_dom * n_shard
    dom, shard = lax.axis_index("dom"), lax.axis_index("shard")
    me = dom * n_shard + shard
    rows, width = feat.shape

    barrier = pltpu.get_barrier_semaphore()

    ring = range(SIDE)
    doms = {
        (dz, dc): lax.rem(dom // 2 + dz, SIDE) * 2 + lax.rem(dom + dc, 2) for dz in ring for dc in range(2)
    }
    shards = {
        (dy, dx): lax.rem(shard // SIDE + dy, SIDE) * SIDE + lax.rem(shard + dx, SIDE)
        for dy in ring
        for dx in ring
    }

    def away(at):
        return sum(min(d, SIDE - d) for d in (at[0][0], *at[1]))

    partners = [(a, b) for a in doms for b in shards if (a, b) != ((0, 0), (0, 0))]
    partners = [(doms[a], shards[b]) for a, b in sorted(partners, key=away, reverse=True)]
    for p in partners:
        pl.semaphore_signal(barrier, inc=1, device_id=p, device_id_type=MESH)
    loads = [
        pltpu.make_async_copy(src, dst, load_sem.at[i])
        for i, (src, dst) in enumerate(
            [(tiles_any, tiles), (attn_any, attn), (fin_any, fin), (fout_any, fout)]
        )
    ]
    for load in loads:
        load.start()

    n_pick = picks.shape[1]
    n_edge = border.shape[1]
    pickf = picks[0].astype(F32).astype(BF16)
    span = BLOCK * n_edge
    lane = iota((n_pick, span), 1)
    spread = onehot(lax.rem(lane // n_edge, n_pick) == iota((n_pick, span), 0))
    chosen = lax.dot_general(
        pickf, spread, (((0,), (0,)), ((), ())), preferred_element_type=F32
    ).astype(I32)
    chosen = onehot(chosen == lax.rem(iota((n, span), 1), n_edge))
    for g in range(n * BLOCK // 256):
        shape = (256, n)
        repeat = onehot(iota(shape, 0) // BLOCK + g * (256 // BLOCK) == iota(shape, 1))
        shape = (256, span)
        keep = iota(shape, 1) // n_edge == lax.rem(iota(shape, 0), BLOCK)
        psend[g * 256 : (g + 1) * 256, :] = jnp.where(keep, dot(repeat, chosen), 0.0).astype(BF16)

    slots, size = tiles.shape[1], tiles.shape[2]
    row_tiles, col_tiles = adj.shape[0] // size, adj.shape[1] // size
    at = coords[0, 0:1, :] * col_tiles + coords[0, 1:2, :]
    lane = iota((1, slots), 1)
    at = jnp.where(lane < count[0, 0], at, col_tiles * col_tiles + lane).astype(F32)
    shape = (slots, slots)
    row, col = iota(shape, 0), iota(shape, 1)
    at_col = jnp.sum(jnp.where(row == col, at, 0.0), 1, keepdims=True)
    slot = (row + 1).astype(F32)
    before = jnp.max(jnp.where((at_col == at) & (row < col), slot, 0.0), 0, keepdims=True)
    final = jnp.max(jnp.where(at_col == col.astype(F32), slot, 0.0), 0, keepdims=True)
    link[...] = jnp.zeros(link.shape, I32)
    link[0:1, 0:slots] = before.astype(I32)
    link[1:2, 0:slots] = final.astype(I32)
    to_scalars = pltpu.make_async_copy(link, link_at, link_sem)
    to_scalars.start()

    def edge_of(index_rows):
        at = jnp.zeros((n_edge, rows), I32)
        for b in range(n_edge):
            at = jnp.where(iota((n_edge, rows), 0) == b, border[0, b], at)
        hit = jnp.where(at == index_rows, 1.0, 0.0)
        return jnp.concatenate([hit] * (span // n_edge), 0).astype(BF16)

    def diagonal(x, f):
        step = span // EACH
        return jnp.concatenate(
            [
                x[c * step : (c + 1) * step, (f * EACH + c) * LANES : (f * EACH + c + 1) * LANES]
                for c in range(EACH)
            ],
            0,
        )

    def post(r, f, edge):
        edge = edge.astype(BF16)
        for g in range(n * BLOCK // 256):
            block = dot(psend[g * 256 : (g + 1) * 256, :], edge)
            send[r, f, g * (256 // BLOCK) : (g + 1) * (256 // BLOCK)] = block.reshape(
                256 // BLOCK, BLOCK, LANES
            ).astype(BF16)

        for p in partners:
            pltpu.make_async_remote_copy(
                src_ref=send.at[r, f, p[0] * n_shard + p[1]],
                dst_ref=recv.at[r, f, me],
                send_sem=send_sem.at[r, f],
                recv_sem=recv_sem.at[r, f],
                device_id=p,
                device_id_type=MESH,
            ).start()
        pltpu.make_async_copy(send.at[r, f, me], recv.at[r, f, me], recv_sem.at[r, f]).start()

    first = dot(edge_of(iota((n_edge, rows), 1)), feat[...])
    pl.semaphore_wait(barrier, n - 1)
    for f in range(HALVES):
        post(0, f, diagonal(first, f))

    to_scalars.wait()
    loads[0].wait()
    total[0] = jnp.zeros((size, size), F32)

    def gather_slot(t, carry):
        total[t + 1] = total[jnp.clip(link_at[0, t], 0, slots)] + tiles[0, t].astype(F32)
        return carry

    lax.fori_loop(0, slots, gather_slot, 0)
    for r in range(row_tiles):
        for c in range(col_tiles):
            adj[r * size : (r + 1) * size, c * size : (c + 1) * size] = total[
                jnp.clip(link_at[1, r * col_tiles + c], 0, slots)
            ].astype(BF16)

    place_t = onehot(iota((rows, rows), 0) == order[...])
    place = place_t.astype(F32).T.astype(BF16)
    hops[0] = dot(place, feat[...]).astype(BF16)
    adj_own[...] = dot(dot(place, adj[:, :rows]).astype(BF16), place_t).astype(BF16)
    adj_halo[...] = dot(place, adj[:, rows:]).astype(BF16)
    edge = edge_of(order[...])
    own_edge[...] = dot(edge, adj_own[...]).astype(BF16)
    halo_part = dot(edge, adj_halo[...]).astype(BF16)
    group = LANES // n_pick
    shape = (LANES, LANES * EACH)
    widen = onehot(
        (iota(shape, 0) // n_pick == iota(shape, 1) // BLOCK)
        & (lax.rem(iota(shape, 0), n_pick) == lax.rem(iota(shape, 1), n_pick))
    )
    shape = (span, LANES * EACH)
    same = iota(shape, 0) // (span // EACH) == lax.rem(iota(shape, 1) // n_pick, EACH)
    for g in range(n // group):
        wide = dot(halo_part[:, g * LANES : (g + 1) * LANES], widen)
        halo_edge[:, g * LANES * EACH : (g + 1) * LANES * EACH] = jnp.where(same, wide, 0.0).astype(BF16)

    def source(i):
        head = lax.rem(i // (LANES // HEADS), HEADS)
        return head * (width // HEADS) + (i // LANES) * (LANES // HEADS) + lax.rem(i, LANES // HEADS)

    shape = (width, width)
    by_row = onehot(iota(shape, 1) == source(iota(shape, 0)))
    by_col = onehot(iota(shape, 0) == source(iota(shape, 1)))
    loads[1].wait()
    for i in range(3):
        attn[0, i] = dot(attn[0, i], by_col).astype(BF16)
    attn[0, 3] = dot(by_row, attn[0, 3]).astype(BF16)

    per = 256 // BLOCK
    shape = (256, 256)
    row, col = iota(shape, 0), iota(shape, 1)
    regroup = onehot(
        (lax.rem(row // n_pick, per) == col // BLOCK)
        & (row // (256 // EACH) == lax.rem(col // n_pick, EACH))
        & (lax.rem(row, n_pick) == lax.rem(col, n_pick))
    )

    shape = (2 * LANES, 2 * LANES)
    seg = LANES // HEADS
    gather = jnp.where(
        iota(shape, 0) // seg == iota(shape, 1) // seg, (width // HEADS) ** -0.5, 0.0
    ).astype(BF16)

    def lanes(c):
        return slice(c * LANES, (c + 1) * LANES)

    def project(h):
        for b in range(rows // 256):
            at = slice(b * 256, (b + 1) * 256)
            a = layer_norm(hops[h, at, :].astype(F32), gain[0, 0:1, :]).astype(BF16)
            q[h, at, :] = dot(a, attn[0, 0]).astype(BF16)
            k[h, at, :] = dot(a, attn[0, 1]).astype(BF16)
            v[h, at, :] = dot(a, attn[0, 2])

        def against(j, carry):
            for b in range(rows // CHUNK):
                at = slice(b * CHUNK, (b + 1) * CHUNK)

                def product(x, y):
                    p = [q[x, at, lanes(c)] * k[y, at, lanes(c)] for c in range(PARTS)]
                    return (p[0] + p[1]) + (p[2] + p[3])

                score[h, j, at, :] = dot(jnp.concatenate([product(h, j), product(j, h)], 1), gather)
            return carry

        lax.fori_loop(0, h + 1, against, 0)

    def arrived(r, f):
        pltpu.make_async_copy(recv.at[r, f], recv.at[r, f], recv_sem.at[r, f]).wait()
        return recv[r, f].astype(F32).reshape(n * BLOCK, LANES).astype(BF16)

    def advance(r, f, got):
        part = 256 // EACH
        for g in range(n * BLOCK // 512):
            both = jnp.concatenate([got[g * 512 : g * 512 + 256], got[g * 512 + 256 : (g + 1) * 512]], 1)
            moved = dot(regroup, both).astype(BF16)
            for c in range(EACH):
                for d in range(2):
                    halo[f, (2 * g + d) * part : (2 * g + d + 1) * part, lanes(c)] = moved[
                        c * part : (c + 1) * part, lanes(d)
                    ]
        at = slice(f * EACH * LANES, (f + 1) * EACH * LANES)
        hops[r + 1, :, at] = (own[:, at] + dot(adj_halo[...], halo[f])).astype(BF16)

    def prepare(r):
        own[...] = dot(adj_own[...], hops[r])
        project(r)

    def hop(r, carry):
        own_part = dot(own_edge[...], hops[r])
        for f in range(HALVES):
            own_diag[f] = diagonal(own_part, f)
        prepare(r)
        for f in range(HALVES):
            got = arrived(r, f)
            post(r + 1, f, own_diag[f] + dot(halo_edge[...], got))
            advance(r, f, got)
        return carry

    lax.fori_loop(0, HOPS - 1, hop, 0)
    prepare(HOPS - 1)
    for f in range(HALVES):
        advance(HOPS - 1, f, arrived(HOPS - 1, f))
    project(HOPS)
    loads[2].wait()
    loads[3].wait()

    share = rows // n_shard
    n_chunk = rows // CHUNK
    side = CHUNK // share

    def chunk_at(step):
        return lax.rem(shard // side + (2, 3, 1, 0)[step], n_chunk)

    def mix(step):
        base = chunk_at(step) * CHUNK
        for b in range(CHUNK // SUB):
            at = pl.ds(pl.multiple_of(base + b * SUB, SUB), SUB)
            for i in range(TOKENS):
                s = [
                    score[max(i, j), min(i, j), at, lanes(0 if i >= j else 1)]
                    for j in range(TOKENS)
                ]
                top = functools.reduce(jnp.maximum, s)
                e = [jnp.exp(x - top) for x in s]
                scale = 1.0 / functools.reduce(jnp.add, e)
                w = [x * scale for x in e]
                to = slice(i * CHUNK + b * SUB, i * CHUNK + (b + 1) * SUB)
                for c in range(PARTS):
                    acc = w[0] * v[0, at, lanes(c)]
                    for j in range(1, TOKENS):
                        acc += w[j] * v[j, at, lanes(c)]
                    ctx[step % 2, to, lanes(c)] = acc.astype(BF16)

    def layer(step):
        at_chunk = chunk_at(step)
        base = at_chunk * CHUNK
        at = pl.ds(pl.multiple_of(base, CHUNK), CHUNK)
        if step + 1 < n_chunk:
            mix(step + 1)
        two = step % 2
        hid[two] = dot(ctx[two], attn[0, 3])
        for i in range(TOKENS):
            to = slice(i * CHUNK, (i + 1) * CHUNK)
            h = hops[i, at, :].astype(F32) + hid[two, to, :]
            hid[two, to, :] = h
            norm[two, to, :] = layer_norm(h, gain[0, 1:2, :]).astype(BF16)
        for b in range(mid.shape[2] // 256):
            x = dot(norm[two], fin[0, :, b * 256 : (b + 1) * 256])
            mid[two, :, b * 256 : (b + 1) * 256] = jax.nn.gelu(x, approximate=True).astype(BF16)
        hid[two] += dot(mid[two], fout[0])

        z0 = hid[two, 0:CHUNK, :]
        base_score = jnp.sum(z0 * readw[0:1, :], -1, keepdims=True)
        s = [
            base_score + jnp.sum(hid[two, i * CHUNK : (i + 1) * CHUNK, :] * readw[1:2, :], -1, keepdims=True)
            for i in range(1, TOKENS)
        ]
        top = functools.reduce(jnp.maximum, s)
        e = [jnp.exp(x - top) for x in s]
        scale = 1.0 / functools.reduce(jnp.add, e)
        state = z0
        for i in range(1, TOKENS):
            state += (e[i - 1] * scale) * hid[two, i * CHUNK : (i + 1) * CHUNK, :]
        stage[at, :] = state.astype(BF16)

        dst = out.at[pl.ds(pl.multiple_of(shard * share, share), share)]
        for far in (2, 3, 1, 0):
            to = at_chunk * side + lax.rem(lax.rem(shard, side) + far, side)
            src = stage.at[pl.ds(pl.multiple_of(to * share, share), share)]
            if step == n_chunk - 1 and far == 0:
                pltpu.make_async_copy(src, dst, out_recv_sem).start()
            else:
                pltpu.make_async_remote_copy(
                    src_ref=src,
                    dst_ref=dst,
                    send_sem=out_send_sem,
                    recv_sem=out_recv_sem,
                    device_id=(dom, to),
                    device_id_type=MESH,
                ).start()

    mix(0)
    for step in range(n_chunk):
        layer(step)

    sent = send.at[0, 0, pl.ds(0, n - 1)]
    for r in range(HOPS):
        for f in range(HALVES):
            pltpu.make_async_copy(sent, sent, send_sem.at[r, f]).wait()
    sent = stage.at[pl.ds(0, rows - share)]
    pltpu.make_async_copy(sent, sent, out_send_sem).wait()
    pltpu.make_async_copy(out, out, out_recv_sem).wait()


def local(
    features,
    tile_values,
    tile_coords,
    tile_count,
    boundary_index,
    peer_pick,
    shuffle_order,
    attn_weight,
    ffn_in,
    ffn_out,
    norm_gain,
    read_weight,
):
    rows, width = features.shape
    size = tile_values.shape[2]
    n, n_pick = peer_pick.shape[1], peer_pick.shape[2]
    halo_rows = n * n_pick
    hidden = ffn_in.shape[2]
    vmem = pl.BlockSpec(memory_space=pltpu.VMEM)
    smem = pl.BlockSpec(memory_space=pltpu.SMEM)
    hbm = pl.BlockSpec(memory_space=pl.ANY)
    message = n * BLOCK
    span = BLOCK * boundary_index.shape[1]
    states = pl.pallas_call(
        window,
        out_shape=jax.ShapeDtypeStruct((rows, width), BF16),
        in_specs=[vmem, vmem, smem, smem, vmem, vmem, hbm, hbm, hbm, hbm, vmem, vmem],
        out_specs=hbm,
        scratch_shapes=[
            pltpu.VMEM((TOKENS, rows, width), BF16),
            pltpu.VMEM((HOPS, HALVES, n, BLOCK, LANES), BF16),
            pltpu.VMEM((HOPS, HALVES, n, BLOCK, LANES), BF16),
            pltpu.VMEM((message, span), BF16),
            pltpu.VMEM((span, rows), BF16),
            pltpu.VMEM((span, message), BF16),
            pltpu.VMEM((rows, rows), BF16),
            pltpu.VMEM((rows, halo_rows), BF16),
            pltpu.VMEM((HALVES, halo_rows, EACH * LANES), BF16),
            pltpu.VMEM((rows, width), F32),
            pltpu.VMEM((HALVES, span, LANES), F32),
            pltpu.VMEM((TOKENS, rows, width), BF16),
            pltpu.VMEM((TOKENS, rows, width), BF16),
            pltpu.VMEM((TOKENS, rows, width), F32),
            pltpu.VMEM(attn_weight.shape, BF16),
            pltpu.VMEM(ffn_in.shape, BF16),
            pltpu.VMEM(ffn_out.shape, BF16),
            pltpu.VMEM(tile_values.shape, BF16),
            pltpu.VMEM((tile_values.shape[1] + 1, size, size), F32),
            pltpu.VMEM((8, LANES), I32),
            pltpu.SMEM((8, LANES), I32),
            pltpu.VMEM((rows, rows + halo_rows), BF16),
            pltpu.VMEM((TOKENS, TOKENS, rows, 2 * LANES), F32),
            pltpu.VMEM((2, TOKENS * CHUNK, width), BF16),
            pltpu.VMEM((2, TOKENS * CHUNK, width), BF16),
            pltpu.VMEM((2, TOKENS * CHUNK, width), F32),
            pltpu.VMEM((2, TOKENS * CHUNK, hidden), BF16),
            pltpu.VMEM((rows, width), BF16),
            pltpu.SemaphoreType.DMA((HOPS, HALVES)),
            pltpu.SemaphoreType.DMA((HOPS, HALVES)),
            pltpu.SemaphoreType.DMA((4,)),
            pltpu.SemaphoreType.DMA,
            pltpu.SemaphoreType.DMA,
            pltpu.SemaphoreType.DMA,
        ],
        compiler_params=pltpu.CompilerParams(
            collective_id=0, has_side_effects=True, vmem_limit_bytes=56 * 2**20
        ),
        name="window",
    )(
        features,
        jnp.swapaxes(tile_coords, 1, 2),
        tile_count.reshape(1, 1),
        boundary_index,
        jnp.swapaxes(peer_pick, 1, 2),
        shuffle_order,
        tile_values,
        attn_weight,
        ffn_in,
        ffn_out,
        norm_gain,
        read_weight,
    )
    return states


def solution(mesh):
    placed = (
        P(("dom", "shard"), None),
        P(("dom", "shard"), None, None, None),
        P(("dom", "shard"), None, None),
        P(("dom", "shard")),
        P(("dom", "shard"), None),
        P(("dom", "shard"), None, None),
        P(("dom", "shard"), None),
        P(),
        P(),
        P(),
        P(),
        P(),
    )
    return jax.shard_map(
        local, mesh=mesh, in_specs=placed, out_specs=P(("dom", "shard"), None), check_vma=False
    )
```

time: 93.8 us -> 67 us (0.71)
  Pallas kernels: 86.4 us -> 64.3 us
  local copies, waits for them, and re-layouts: 6.43 us -> 1.87 us
    pallas_call x1, Pallas kernels: 85 us -> 64.3 us  [local(): pl.pallas_call(window, out_shape=jax.ShapeDtypeStruct((rows, width), BF16...]
    unnamed x7 -> x1, local copies, waits for them, and re-layouts: 6.43 us -> 1.87 us
    pallas_call x1 -> x0, Pallas kernels: 1.44 us -> none  [local(): pl.pallas_call(build_adjacency, out_shape=jax.ShapeDtypeStruct((rows, row...]
where the time goes in v2:
time: 67 us; the launch traced here: 66.8 us
  Pallas kernels  64.3 us (96%)
  local copies, waits for them, and re-layouts  1.87 us (3%)
    pallas_call x1, Pallas kernels, local(): pl.pallas_call(window, out_shape=jax.ShapeDtypeStruct((rows, width), BF16...  64.3 us
    unnamed x1, local copies, waits for them, and re-layouts  1.87 us

profile of v2, /device:TPU:1, one launch (start us, length us, event | category | flops | bytes accessed | tf_op | source)
XLA Modules:
  0.0 66.8 jit_solution(3491680259589814203)
XLA Ops:
  0.7 64.3 %window.1 = bf16[512,512]{1,0:T(8,128)(2,1)} custom-call(bf16[512,512]{1,0:T(8,128)(2,1)} %feat.1, s32[1,2,48]{2,1,0:T(2,128)} %bitcast.5, s32[1,1]{1,0:T(1,128)} %bitcast.3.count, s32[1,8]{1,0:T(1,128)} %border.1, s32[1,4,128]{2,1,0:T(4,128)} %bitcast.4, s32[1,512]{1,0:T(1,128)} %order.1, bf16[1,48,128,128]{3,2,1,0:T(8,128)(2,1)} %tiles_any.1, ...), custom_call_target="tpu_custom_call" | custom-call | tf_op jit(solution)/shard_map/window/pallas_call | solution.py:439
  65.0 1.9 %copy.15 = bf16[512,512]{1,0:T(8,128)(2,1)} copy(bf16[512,512]{1,0:T(8,128)(2,1)} %window.1) | data formatting | bytes 1048576

commit v3 on v2

--- a/solution.py
+++ b/solution.py
@@ -331,9 +331,9 @@
     def chunk_at(step):
         return lax.rem(shard // side + (2, 3, 1, 0)[step], n_chunk)
 
-    def mix(step):
+    def mix(step, blocks):
         base = chunk_at(step) * CHUNK
-        for b in range(CHUNK // SUB):
+        for b in blocks:
             at = pl.ds(pl.multiple_of(base + b * SUB, SUB), SUB)
             for i in range(TOKENS):
                 s = [
@@ -351,24 +351,10 @@
                         acc += w[j] * v[j, at, lanes(c)]
                     ctx[step % 2, to, lanes(c)] = acc.astype(BF16)
 
-    def layer(step):
+    def finish(step):
         at_chunk = chunk_at(step)
-        base = at_chunk * CHUNK
-        at = pl.ds(pl.multiple_of(base, CHUNK), CHUNK)
-        if step + 1 < n_chunk:
-            mix(step + 1)
+        at = pl.ds(pl.multiple_of(at_chunk * CHUNK, CHUNK), CHUNK)
         two = step % 2
-        hid[two] = dot(ctx[two], attn[0, 3])
-        for i in range(TOKENS):
-            to = slice(i * CHUNK, (i + 1) * CHUNK)
-            h = hops[i, at, :].astype(F32) + hid[two, to, :]
-            hid[two, to, :] = h
-            norm[two, to, :] = layer_norm(h, gain[0, 1:2, :]).astype(BF16)
-        for b in range(mid.shape[2] // 256):
-            x = dot(norm[two], fin[0, :, b * 256 : (b + 1) * 256])
-            mid[two, :, b * 256 : (b + 1) * 256] = jax.nn.gelu(x, approximate=True).astype(BF16)
-        hid[two] += dot(mid[two], fout[0])
-
         z0 = hid[two, 0:CHUNK, :]
         base_score = jnp.sum(z0 * readw[0:1, :], -1, keepdims=True)
         s = [
@@ -399,9 +385,32 @@
                     device_id_type=MESH,
                 ).start()
 
-    mix(0)
+    def layer(step):
+        at_chunk = chunk_at(step)
+        base = at_chunk * CHUNK
+        at = pl.ds(pl.multiple_of(base, CHUNK), CHUNK)
+        two = step % 2
+        hid[two] = dot(ctx[two], attn[0, 3])
+        if step > 0:
+            finish(step - 1)
+        for i in range(TOKENS):
+            to = slice(i * CHUNK, (i + 1) * CHUNK)
+            h = hops[i, at, :].astype(F32) + hid[two, to, :]
+            hid[two, to, :] = h
+            norm[two, to, :] = layer_norm(h, gain[0, 1:2, :]).astype(BF16)
+        blocks = mid.shape[2] // 256
+        subs = CHUNK // SUB
+        for b in range(blocks):
+            x = dot(norm[two], fin[0, :, b * 256 : (b + 1) * 256])
+            if step + 1 < n_chunk:
+                mix(step + 1, range(b * subs // blocks, (b + 1) * subs // blocks))
+            mid[two, :, b * 256 : (b + 1) * 256] = jax.nn.gelu(x, approximate=True).astype(BF16)
+        hid[two] += dot(mid[two], fout[0])
+
+    mix(0, range(CHUNK // SUB))
     for step in range(n_chunk):
         layer(step)
+    finish(n_chunk - 1)
 
     sent = send.at[0, 0, pl.ds(0, n - 1)]
     for r in range(HOPS):

time: 67 us -> 66.2 us (0.988)
  Pallas kernels: 64.3 us -> 63.5 us
    pallas_call x1, Pallas kernels: 64.3 us -> 63.5 us  [local(): pl.pallas_call(window, out_shape=jax.ShapeDtypeStruct((rows, width), BF16...]
where the time goes in v3:
time: 66.2 us; the launch traced here: 66 us
  Pallas kernels  63.5 us (96%)
  local copies, waits for them, and re-layouts  1.87 us (3%)
    pallas_call x1, Pallas kernels, local(): pl.pallas_call(window, out_shape=jax.ShapeDtypeStruct((rows, width), BF16...  63.5 us
    unnamed x1, local copies, waits for them, and re-layouts  1.87 us

profile of v3, /device:TPU:1, one launch (start us, length us, event | category | flops | bytes accessed | tf_op | source)
XLA Modules:
  0.0 66.0 jit_solution(12732489935749605741)
XLA Ops:
  0.7 63.5 %window.1 = bf16[512,512]{1,0:T(8,128)(2,1)} custom-call(bf16[512,512]{1,0:T(8,128)(2,1)} %feat.1, s32[1,2,48]{2,1,0:T(2,128)} %bitcast.5, s32[1,1]{1,0:T(1,128)} %bitcast.3.count, s32[1,8]{1,0:T(1,128)} %border.1, s32[1,4,128]{2,1,0:T(4,128)} %bitcast.4, s32[1,512]{1,0:T(1,128)} %order.1, bf16[1,48,128,128]{3,2,1,0:T(8,128)(2,1)} %tiles_any.1, ...), custom_call_target="tpu_custom_call" | custom-call | tf_op jit(solution)/shard_map/window/pallas_call | solution.py:448
  64.2 1.9 %copy.15 = bf16[512,512]{1,0:T(8,128)(2,1)} copy(bf16[512,512]{1,0:T(8,128)(2,1)} %window.1) | data formatting | bytes 1048576
